TPU v7x, 32 devices: a whole 2x2x4 slice. The times are simulated.
32 devices in a mesh: pts: 16 (over z, y, core), freq: 2 (over x).
Axes of the slice: x: 2, y: 2, z: 4, core: 2. Of those that a mesh axis runs over, the one named last changes fastest.
Arguments:
- snapshots: float32 [2112, 12288], P(None, ('pts', 'freq')), may hold values from -6 to 6
- weight: float32 [12288], P('pts'), may hold values from 0.1 to 10
- start_vec: float32 [64, 2, 32], replicated, may hold values from -6 to 6
Outputs:
- gram_mine: float32 [64, 2, 32, 32], P('freq')
- modes: float32 [64, 2, 12288], P('freq', None, 'pts')
All inputs are finite; a program needn't handle non-finite values.
Results may differ from a plain program's by a relative error of at most 0.0003.
Values sent between devices are 32-bit elements; how exact they have to be, the bound alone decides.
No kernel may reach another device: no remote copies, remote signals or barrier semaphores. Data moves between devices by JAX's collectives and lax.ppermute only.
A program may use at most 64 MiB of HBM per device.

v0:
```python
import functools
import math

import jax
import jax.numpy as jnp
import numpy as np
from jax import lax
from jax.experimental import pallas as pl
from jax.experimental.pallas import tpu as pltpu
from jax.sharding import PartitionSpec as P

NFFT = 128
HALF = NFFT // 2
NF = 64
NB = 32
LANES = 128
PACK = 4
VMEM_LIMIT = 56 * 1024 * 1024
SMALL_LIMIT = 16 * 1024 * 1024
VMEM = pl.BlockSpec(memory_space=pltpu.VMEM)


def dft_values():
    times = np.arange(NFFT)
    freqs = np.arange(NF)
    phases = (freqs[:, None] * times[None, :] % NFFT) * (2.0 * math.pi / NFFT)
    window = 0.5 - 0.5 * np.cos(times * (2.0 * math.pi / NFFT))
    weighted = window / np.sqrt(np.sum(window * window))
    return np.cos(phases) * weighted, -np.sin(phases) * weighted


def split_table(table):
    high = table.astype(jnp.bfloat16)
    low = (table - high.astype(np.float64)).astype(jnp.bfloat16)
    return high, low


def dft_operand():
    real, imag = dft_values()
    high, low = split_table(np.concatenate([real, imag], axis=0))
    return np.block([[high, high], [low, np.zeros_like(low)]])


def mode_tables():
    real, imag = dft_values()
    order = np.concatenate([np.arange(0, NF, 2), np.arange(1, NF, 2)])
    real, imag = real[order].T, imag[order].T
    first = np.concatenate([real, imag], axis=1)
    second = np.concatenate([-imag, real], axis=1)
    return np.stack([first, second]).astype(np.float32)


def split(value):
    high = value.astype(jnp.bfloat16)
    low = (value - high.astype(jnp.float32)).astype(jnp.bfloat16)
    return high, low


def load_weights(w_ref, col_tiles):
    first = lax.axis_index("freq") * col_tiles
    return jnp.concatenate([w_ref[pl.ds(first + c, 1), :] for c in range(col_tiles)], axis=1)


def near_index():
    return lax.axis_index("freq") * 2 + lax.rem(lax.axis_index("pts"), 2)


def far_index():
    return lax.div(lax.axis_index("pts"), 2)


def gram_kernel(
    total_rows,
    chunks,
    x_hbm,
    w_hbm,
    dft_hbm,
    *refs,
):
    out_refs = refs[:chunks]
    (high_hbm, low_hbm, x_ref, w_ref, dft_ref, high_ref, low_ref, spec_ref, z_ref, pack_ref) = refs[
        chunks:-2
    ]
    in_sems, out_sems = refs[-2:]
    times, cols = x_ref.shape
    halves = times // HALF
    col_tiles = cols // LANES
    pieces = in_sems.shape[0] - 2
    piece = times // pieces

    def fetch(i):
        rows = pl.ds(i * piece, piece)
        return pltpu.make_async_copy(x_hbm.at[rows], x_ref.at[rows], in_sems.at[i])

    fetch_w = pltpu.make_async_copy(w_hbm, w_ref, in_sems.at[pieces])
    fetch_dft = pltpu.make_async_copy(dft_hbm, dft_ref, in_sems.at[pieces + 1])
    for i in range(pieces):
        fetch(i).start()
    fetch_w.start()
    fetch_dft.start()

    acc = jnp.zeros((HALF, cols), jnp.float32)
    for i in range(pieces):
        fetch(i).wait()
        for h in range(piece // HALF):
            acc = acc + x_ref[pl.ds(i * piece + h * HALF, HALF), :]
    mean = jnp.sum(acc, axis=0, keepdims=True) / times
    fetch_w.wait()
    scale = jnp.sqrt(load_weights(w_ref, col_tiles) / (2.0 * total_rows))

    def center(i, carry):
        rows = pl.ds(pl.multiple_of(i * HALF, HALF), HALF)
        high, low = split((x_ref[rows, :] - mean) * scale)
        high_ref[rows, :] = high
        low_ref[rows, :] = low
        return carry

    lax.fori_loop(0, halves, center, 0, unroll=3)
    save_high = pltpu.make_async_copy(high_ref, high_hbm, out_sems.at[0])
    save_low = pltpu.make_async_copy(low_ref, low_hbm, out_sems.at[1])
    save_high.start()
    save_low.start()
    fetch_dft.wait()

    def transform(i, carry):
        blocks = []
        for s in range(2):
            rows = pl.ds(pl.multiple_of((2 * i + s) * HALF, HALF), NFFT)
            blocks.append(jnp.concatenate([high_ref[rows, :], low_ref[rows, :]], axis=0))
        both = jnp.dot(
            dft_ref[...], jnp.concatenate(blocks, axis=1), preferred_element_type=jnp.float32
        )
        spectrum = both[: 2 * NF] + both[2 * NF :]
        for s in range(2):
            for o in range(2 * NF // 8):
                for c in range(col_tiles):
                    first = s * cols + c * LANES
                    spec_ref[c, o, pl.ds(2 * i + s, 8, stride=NB + 1), :] = spectrum[
                        8 * o : 8 * o + 8, first : first + LANES
                    ]
        return carry

    lax.fori_loop(0, NB // 2, transform, 0, unroll=2)

    row = lax.broadcasted_iota(jnp.int32, (NB, LANES), 0)
    lane = lax.broadcasted_iota(jnp.int32, (NB, LANES), 1)
    upper = row <= lane % NB
    lower = row >= lane % NB
    left = lane[: NB // 2] < LANES // 2
    octets = NF // 8
    contract = (((1,), (1,)), ((), ()))

    def correlate(o, carry):
        direct = []
        flipped = []
        for half in range(2):
            for part in range(2):
                for q in range(PACK):
                    first = (NB + 1) * (PACK * half + q)
                    for c in range(col_tiles):
                        value = spec_ref[c, o + octets * part, pl.ds(first, NB), :]
                        high = value.astype(jnp.bfloat16)
                        low = (2.0 * (value - high.astype(jnp.float32))).astype(jnp.bfloat16)
                        rows = pl.ds(part * LANES + q * NB, NB)
                        z_ref[half, rows, pl.ds(c * LANES, LANES)] = high
                        z_ref[half, rows, pl.ds(cols + c * LANES, LANES)] = low
            high = z_ref[half, :, pl.ds(0, cols)]
            product = lax.dot_general(
                jnp.concatenate([high, high], axis=1),
                z_ref[half],
                contract,
                preferred_element_type=jnp.float32,
            )
            gram_real = jnp.zeros((NB, LANES), jnp.float32)
            gram_imag = jnp.zeros((NB, LANES), jnp.float32)
            for q in range(PACK):
                mine = lane // NB == q
                real = product[q * NB : (q + 1) * NB]
                imag = product[LANES + q * NB : LANES + (q + 1) * NB]
                gram_real = jnp.where(mine, real[:, :LANES] + imag[:, LANES:], gram_real)
                gram_imag = jnp.where(mine, real[:, LANES:] - imag[:, :LANES], gram_imag)
            direct.append(jnp.where(upper, gram_real, gram_imag))
            flipped.append(jnp.where(lower, gram_real, -gram_imag))
        turned = jnp.concatenate(flipped + flipped, axis=0).T
        for half in range(2):
            packed = direct[half]
            for q in range(PACK):
                block = turned[q * NB : (q + 1) * NB]
                shift = (q - half) % PACK
                if shift:
                    block = pltpu.roll(block, shift * NB, 1)
                packed = packed + jnp.where(lane // NB == q, block, 0.0)
            top = packed[: NB // 2]
            bottom = packed[NB // 2 :]
            pair = 4 * o + 2 * half
            pack_ref[pair] = jnp.where(left, top, pltpu.roll(bottom, LANES // 2, 1))
            pack_ref[pair + 1] = jnp.where(left, pltpu.roll(top, LANES // 2, 1), bottom)
        return carry

    lax.fori_loop(0, octets, correlate, 0)
    length = NF // 2 // chunks
    for m in range(chunks):
        source = near_index() ^ m if chunks > 1 else 0
        out_refs[m][...] = pack_ref[pl.ds(source * length, length)]
    save_high.wait()
    save_low.wait()


def gram_parts(snapshots, weight_rows, total_rows, chunks):
    times, cols = snapshots.shape
    dft = dft_operand()
    pieces = 11
    any_space = pl.BlockSpec(memory_space=pltpu.HBM)
    part = jax.ShapeDtypeStruct((NF // 2 // chunks, NB // 2, LANES), jnp.float32)
    saved = jax.ShapeDtypeStruct((times, cols), jnp.bfloat16)
    results = pl.pallas_call(
        functools.partial(gram_kernel, total_rows, chunks),
        out_shape=(part,) * chunks + (saved,) * 2,
        in_specs=[any_space] * 3,
        out_specs=(VMEM,) * chunks + (any_space,) * 2,
        scratch_shapes=[
            pltpu.VMEM((times, cols), jnp.float32),
            pltpu.VMEM(weight_rows.shape, jnp.float32),
            pltpu.VMEM(dft.shape, jnp.bfloat16),
            pltpu.VMEM((times, cols), jnp.bfloat16),
            pltpu.VMEM((times, cols), jnp.bfloat16),
            pltpu.VMEM((cols // LANES, 2 * NF // 8, 8 * (NB + 1), LANES), jnp.float32),
            pltpu.VMEM((2, 2 * LANES, 2 * cols), jnp.bfloat16),
            pltpu.VMEM((NF // 2, NB // 2, LANES), jnp.float32),
            pltpu.SemaphoreType.DMA((pieces + 2,)),
            pltpu.SemaphoreType.DMA((2,)),
        ],
        compiler_params=pltpu.CompilerParams(vmem_limit_bytes=VMEM_LIMIT),
        cost_estimate=pl.CostEstimate(
            flops=5_000_000_000, bytes_accessed=8_000_000, transcendentals=0
        ),
        name="gram_parts",
    )(snapshots, weight_rows, jnp.asarray(dft))
    return results[:chunks], results[chunks], results[chunks + 1]


def hermitian_pair(packed):
    square = jnp.concatenate([packed, pltpu.roll(packed, LANES // 2, 1)], axis=0)
    tall = jnp.concatenate([square] * (LANES // NB), axis=0).T
    row = lax.broadcasted_iota(jnp.int32, (NB, LANES), 0)
    lane = lax.broadcasted_iota(jnp.int32, (NB, LANES), 1)
    flipped = jnp.where(lane // NB == 0, tall[:NB], tall[NB : 2 * NB])
    col = lane % NB
    real = jnp.where(row <= col, square, flipped)
    imag = jnp.where(row > col, square, jnp.where(row < col, -flipped, 0.0))
    return real, imag, lane


def small_call(kernel, name, out_shape, scratch_shapes=(), limit=SMALL_LIMIT):
    def call(*args):
        return pl.pallas_call(
            kernel,
            out_shape=out_shape,
            in_specs=[VMEM] * len(args),
            out_specs=VMEM if isinstance(out_shape, jax.ShapeDtypeStruct) else (VMEM,) * len(out_shape),
            scratch_shapes=list(scratch_shapes),
            compiler_params=pltpu.CompilerParams(vmem_limit_bytes=limit),
            name=name,
        )(*args)

    return call


def floats(*shape):
    return jax.ShapeDtypeStruct(shape, jnp.float32)


def near_sum_kernel(*refs):
    parts, outs, sum_ref = refs[:4], refs[4:-1], refs[-1]
    sum_ref[...] = (parts[0][...] + parts[1][...]) + (parts[2][...] + parts[3][...])
    for n, out in enumerate(outs):
        out[...] = sum_ref[far_index() ^ n]


def far_sum_kernel(*refs):
    parts, start_ref, out_ref = refs[:-2], refs[-2], refs[-1]
    packed = parts[0][...]
    for part in parts[1:]:
        packed = packed + part[...]
    out_ref[pl.ds(0, NB // 2), :] = packed
    real, imag, lane = hermitian_pair(packed)
    start_real = start_ref[0]
    start_imag = start_ref[1]
    resp_real = jnp.sum(real * start_real + imag * start_imag, axis=0, keepdims=True)
    resp_imag = jnp.sum(real * start_imag - imag * start_real, axis=0, keepdims=True)
    power = resp_real * resp_real + resp_imag * resp_imag
    lane = lane[:1]
    first = jnp.sum(jnp.where(lane < NB, power, 0.0), axis=1, keepdims=True) / NB
    second = (
        jnp.sum(jnp.where((lane >= NB) & (lane < 2 * NB), power, 0.0), axis=1, keepdims=True) / NB
    )
    scaling = 1.0 / jnp.sqrt(jnp.where(lane < NB, first, second) + 1e-06)
    resp = jnp.where(
        lane < LANES // 2, resp_real * scaling, pltpu.roll(resp_imag * scaling, LANES // 2, 1)
    )
    out_ref[pl.ds(NB // 2, 8), :] = jnp.broadcast_to(resp, (8, LANES))


def far_join_kernel(*refs):
    parts, resp_ref, packed_ref = refs[:-2], refs[-2], refs[-1]
    for n, part in enumerate(parts):
        place = far_index() ^ n
        resp_ref[pl.ds(place, 1), :] = part[pl.ds(NB // 2, 1), :]
        packed_ref[place] = part[pl.ds(0, NB // 2), :]


def unpack_kernel(*refs):
    parts, out_ref = refs[:-1], refs[-1]
    own = lax.rem(lax.axis_index("pts"), 2)
    count = parts[0].shape[0]
    for m, part in enumerate(parts):
        first = (own ^ m) * 2 * count if len(parts) > 1 else 0
        for i in range(count):
            real, imag, _ = hermitian_pair(part[i])
            for q in range(2):
                out_ref[first + 2 * i + q, 0] = real[:, q * NB : (q + 1) * NB]
                out_ref[first + 2 * i + q, 1] = imag[:, q * NB : (q + 1) * NB]


def unpack_gram(*parts):
    pairs = sum(part.shape[0] for part in parts)
    return small_call(unpack_kernel, "unpack_gram", floats(2 * pairs, 2, NB, NB))(*parts)


def modes_kernel(total_rows, n_resp, *refs):
    high_hbm, low_hbm, w_ref, table_ref = refs[:4]
    resp_refs = refs[4 : 4 + n_resp]
    out_ref, resp_ref, resp_t, a_ref, x_ref, sems = refs[4 + n_resp :]
    times, cols = high_hbm.shape
    padded = x_ref.shape[1]
    pairs = NF // 2
    fetches = [
        pltpu.make_async_copy(source, x_ref.at[i, pl.ds(0, times)], sems.at[i])
        for i, source in enumerate((high_hbm, low_hbm))
    ]
    for fetch in fetches:
        fetch.start()
    if padded > times:
        pad = pl.ds(times, padded - times)
        x_ref[0, pad, :] = jnp.zeros((padded - times, cols), jnp.bfloat16)
        x_ref[1, pad, :] = jnp.zeros((padded - times, cols), jnp.bfloat16)
    count = pairs // n_resp
    for m, part in enumerate(resp_refs):
        place = (near_index() ^ m) * count if n_resp > 1 else 0
        resp_ref[pl.ds(place, count), :] = part[...]
    tall = jnp.concatenate([resp_ref[...]] * (LANES // pairs), axis=0).T
    lane = lax.broadcasted_iota(jnp.int32, (NB, LANES), 1)
    turned = tall[:NB]
    for q in range(1, PACK):
        turned = jnp.where(lane // pairs == q, tall[q * NB : (q + 1) * NB], turned)
    swapped = pltpu.roll(turned, LANES // 2, 1)
    left = lane < LANES // 2
    resp_t[0] = jnp.where(left, turned, swapped)
    resp_t[1] = jnp.where(left, swapped, turned)
    for j in range(padded // HALF):
        value = jnp.zeros((HALF, LANES), jnp.float32)
        for block, start in ((j, 0), (j - 1, HALF)):
            if 0 <= block < NB:
                for part in range(2):
                    value += resp_t[part, pl.ds(block, 1), :] * table_ref[part, pl.ds(start, HALF), :]
        high, low = split(value)
        a_ref[0, pl.ds(j * HALF, HALF), :] = high
        a_ref[1, pl.ds(j * HALF, HALF), :] = low
    dot = functools.partial(
        lax.dot_general,
        dimension_numbers=(((0,), (0,)), ((), ())),
        preferred_element_type=jnp.float32,
    )
    for fetch in fetches:
        fetch.wait()
    modes = dot(a_ref[0], x_ref[0]) + dot(a_ref[0], x_ref[1]) + dot(a_ref[1], x_ref[0])
    modes = modes * jnp.sqrt(2.0 * total_rows / load_weights(w_ref, cols // LANES))
    n_freq = out_ref.shape[0]
    mine = pairs // n_freq
    group = lax.axis_index("freq")
    for part in range(2):
        for parity in range(2):
            for f in range(n_freq):
                first = (2 * part + parity) * pairs + f * mine
                slot = f ^ group if n_freq == 2 else f
                for c in range(cols // LANES):
                    out_ref[slot, 2 * c + part, pl.ds(parity, mine, stride=2), :] = modes[
                        first : first + mine, c * LANES : (c + 1) * LANES
                    ]


def local_modes(high, low, weight_rows, responses, total_rows, n_freq):
    times, cols = high.shape
    padded = -(-times // 256) * 256
    any_space = pl.BlockSpec(memory_space=pltpu.HBM)
    n_resp = len(responses)
    return pl.pallas_call(
        functools.partial(modes_kernel, total_rows, n_resp),
        out_shape=floats(n_freq, 2 * cols // LANES, NF // n_freq, LANES),
        in_specs=[any_space] * 2 + [VMEM] * (2 + n_resp),
        out_specs=VMEM,
        scratch_shapes=[
            pltpu.VMEM((NF // 2, LANES), jnp.float32),
            pltpu.VMEM((2, NB, LANES), jnp.float32),
            pltpu.VMEM((2, padded, LANES), jnp.bfloat16),
            pltpu.VMEM((2, padded, cols), jnp.bfloat16),
            pltpu.SemaphoreType.DMA((2,)),
        ],
        compiler_params=pltpu.CompilerParams(vmem_limit_bytes=SMALL_LIMIT),
        name="local_modes",
    )(high, low, weight_rows, jnp.asarray(mode_tables()), *responses)


def join_kernel(kept_ref, got_ref, out_ref):
    tiles = got_ref.shape[0] // 2
    group = lax.axis_index("freq")
    for slot, ref in enumerate((kept_ref.at[0], got_ref)):
        for c in range(tiles):
            lanes = pl.ds(pl.multiple_of(((group ^ slot) * tiles + c) * LANES, LANES), LANES)
            for part in range(2):
                out_ref[:, part, lanes] = ref[2 * c + part]


def join_modes(kept, got):
    tiles, count, _ = got.shape
    return small_call(join_kernel, "join_modes", floats(count, 2, tiles * LANES))(kept, got)


def response_of(gram, start_vec):
    matvec = functools.partial(jnp.einsum, "fjk,fk->fj", precision=lax.Precision.HIGHEST)
    resp_real = matvec(gram[:, 0], start_vec[:, 0]) - matvec(gram[:, 1], start_vec[:, 1])
    resp_imag = matvec(gram[:, 0], start_vec[:, 1]) + matvec(gram[:, 1], start_vec[:, 0])
    scaling = 1.0 / jnp.sqrt(
        jnp.mean(resp_real * resp_real + resp_imag * resp_imag, axis=1, keepdims=True) + 1e-06
    )
    return jnp.stack([resp_real * scaling, resp_imag * scaling], axis=1)


def swap(value, mask, n_devices):
    return lax.ppermute(value, ("pts", "freq"), [(i, i ^ mask) for i in range(n_devices)])


def two_level_shards(n_devices, snapshots, weight, start_vec):
    total_rows = float(weight.shape[0] * 16)
    weight_rows = weight.reshape(-1, LANES)
    parts, high, low = gram_parts(snapshots, weight_rows, total_rows, 4)
    near = (0, 2, 1, 3)
    far = tuple(4 * n for n in range(8))

    first = (near_index() * 8 + far_index()) * 2
    start_pair = lax.dynamic_slice_in_dim(start_vec, first, 2, 0)
    start_pair = jnp.transpose(start_pair, (1, 2, 0))[:, :, :, None]
    start_pair = jnp.broadcast_to(start_pair, (2, NB, 2, NB)).reshape(2, NB, 2 * NB)
    start_pair = jnp.concatenate([start_pair, start_pair], axis=2)

    got = [parts[0]] + [swap(parts[m], near[m], n_devices) for m in range(1, 4)]
    parts = small_call(
        near_sum_kernel,
        "near_sum",
        (floats(NB // 2, LANES),) * 8,
        [pltpu.VMEM((8, NB // 2, LANES), jnp.float32)],
    )(*got)
    got = [parts[0]] + [swap(parts[n], far[n], n_devices) for n in range(1, 8)]
    own = small_call(far_sum_kernel, "far_sum", floats(NB // 2 + 8, LANES))(*got, start_pair)
    got = [own] + [swap(own, far[n], n_devices) for n in range(1, 8)]
    response, packed = small_call(
        far_join_kernel, "far_join", (floats(8, LANES), floats(8, NB // 2, LANES))
    )(*got)
    responses = [response] + [swap(response, near[m], n_devices) for m in range(1, 4)]
    gram_mine = unpack_gram(packed, swap(packed, near[1], n_devices))
    modes = local_modes(high, low, weight_rows, responses, total_rows, 2)
    modes = join_modes(modes, swap(modes[1], 1, n_devices))
    return gram_mine, modes


def shards(n_pts, n_freq, snapshots, weight, start_vec):
    cols = snapshots.shape[1]
    total_rows = float(weight.shape[0] * n_pts)
    n_devices = n_pts * n_freq
    mine_count = NF // n_freq
    group = lax.axis_index("freq")
    weight_rows = weight.reshape(-1, LANES)
    (parts,), high, low = gram_parts(snapshots, weight_rows, total_rows, 1)
    share = parts.reshape(n_devices, -1)
    share = jnp.sum(lax.all_to_all(share, ("freq", "pts"), 0, 0, tiled=True), axis=0)
    packed = lax.all_gather(share, "pts", axis=0, tiled=True)
    gram_mine = unpack_gram(packed.reshape(mine_count // 2, NB // 2, LANES))
    start_mine = lax.dynamic_slice_in_dim(start_vec, group * mine_count, mine_count, 0)
    response = lax.all_gather(response_of(gram_mine, start_mine), "freq", axis=0, tiled=True)
    response = jnp.transpose(response.reshape(NF // 2, 2, 2, NB), (0, 2, 1, 3))
    response = response.reshape(NF // 2, LANES)
    modes = local_modes(high, low, weight_rows, (response,), total_rows, n_freq)
    modes = lax.all_to_all(modes, "freq", 0, 0, tiled=True)
    modes = modes.reshape(n_freq, cols // LANES, 2, mine_count, LANES)
    modes = jnp.transpose(modes, (3, 2, 0, 1, 4)).reshape(mine_count, 2, n_freq * cols)
    return gram_mine, modes


def solution(mesh):
    n_pts, n_freq = mesh.shape["pts"], mesh.shape["freq"]
    if (n_pts, n_freq) == (16, 2):
        body = functools.partial(two_level_shards, n_pts * n_freq)
    else:
        body = functools.partial(shards, n_pts, n_freq)
    placed = (P(None, ("pts", "freq")), P("pts"), P())
    return jax.shard_map(
        body,
        mesh=mesh,
        in_specs=placed,
        out_specs=(P("freq", None, None, None), P("freq", None, "pts")),
        check_vma=False,
    )
```

profile of v0, /device:TPU:0, one launch (start us, length us, event | category | flops | bytes accessed | tf_op | source)
XLA Modules:
  0.0 67.6 jit_solution(11898780475305268649)
XLA Ops:
  0.6 0.0 copy-start
  0.6 0.0 copy-start.3
  0.7 12.2 %gram_parts.1 = (f32[8,16,128]{2,1,0:T(8,128)}, f32[8,16,128]{2,1,0:T(8,128)}, f32[8,16,128]{2,1,0:T(8,128)}, f32[8,16,128]{2,1,0:T(8,128)}, bf16[2112,384]{1,0:T(8,128)(2,1)}, /*index=5*/bf16[2112,384]{1,0:T(8,128)(2,1)}) custom-call(f32[2112,384]{1,0:T(8,128)} %x_hbm.1, f32[6,128]{1,0:T(8,128)} %bitcast.5, bf16[256,256]{1,0:T(8,128)(2,1)} %constant.25.clone.dft_hbm), custom_call_target="tpu_custom_call" | custom-call | flops 5000000000 | bytes 8000000 | tf_op jit(solution)/shard_map/gram_parts/pallas_call | solution.py:216
  12.9 0.5 collective-permute-start
  13.4 2.6 %collective-permute-start.1 = (f32[8,16,128]{2,1,0:T(8,128)}, f32[8,16,128]{2,1,0:T(8,128)S(1)}, u32[]{:S(2)}, u32[]{:S(2)}) collective-permute-start(f32[8,16,128]{2,1,0:T(8,128)} %get-tuple-element.20), channel_id=1, source_target_pairs={{0,1},{1,0},{2,3},{3,2},{4,5},{5,4},{6,7},{7,6},{8,9},{9,8},{10,11... | collective-permute-start | bytes 196616 | tf_op jit(solution)/shard_map/ppermute | solution.py:440
  16.0 0.1 collective-permute-start.2
  16.1 0.0 collective-permute-done.refs_1_
  16.1 2.8 %collective-permute-done.1.refs_2_ = f32[8,16,128]{2,1,0:T(8,128)S(1)} collective-permute-done((f32[8,16,128]{2,1,0:T(8,128)}, f32[8,16,128]{2,1,0:T(8,128)S(1)}, u32[]{:S(2)}, u32[]{:S(2)}) %collective-permute-start.1) | collective-permute-done | bytes 65568 | tf_op jit(solution)/shard_map/ppermute | solution.py:440
  18.9 1.4 %collective-permute-done.2.refs_3_ = f32[8,16,128]{2,1,0:T(8,128)S(1)} collective-permute-done((f32[8,16,128]{2,1,0:T(8,128)}, f32[8,16,128]{2,1,0:T(8,128)S(1)}, u32[]{:S(2)}, u32[]{:S(2)}) %collective-permute-start.2) | collective-permute-done | bytes 65568 | tf_op jit(solution)/shard_map/ppermute | solution.py:440
  20.3 0.8 %copy-done.4 = f32[8,16,128]{2,1,0:T(8,128)S(1)} copy-done((f32[8,16,128]{2,1,0:T(8,128)S(1)}, f32[8,16,128]{2,1,0:T(8,128)}, u32[]{:S(2)}) %copy-start.4) | copy-done | bytes 65560
  21.2 1.6 %collective-permute-start.3 = (f32[16,128]{1,0:T(8,128)S(1)}, f32[16,128]{1,0:T(8,128)S(1)}, u32[]{:S(2)}, u32[]{:S(2)}) collective-permute-start(f32[16,128]{1,0:T(8,128)S(1)} %get-tuple-element.23), channel_id=1, source_target_pairs={{0,4},{1,5},{2,6},{3,7},{4,0},{5,1},{6,2},{7,3},{8,12},{9,13},{10,... | collective-permute-start | bytes 24584 | tf_op jit(solution)/shard_map/ppermute | solution.py:440
  22.8 1.6 %collective-permute-start.4 = (f32[16,128]{1,0:T(8,128)S(1)}, f32[16,128]{1,0:T(8,128)S(1)}, u32[]{:S(2)}, u32[]{:S(2)}) collective-permute-start(f32[16,128]{1,0:T(8,128)S(1)} %get-tuple-element.24), channel_id=1, source_target_pairs={{0,8},{1,9},{2,10},{3,11},{4,12},{5,13},{6,14},{7,15},{8,0},{9,1},... | collective-permute-start | bytes 24584 | tf_op jit(solution)/shard_map/ppermute | solution.py:440
  24.4 0.1 dynamic-slice_bitcast_fusion
  24.4 0.1 broadcast_in_dim.2
  24.6 0.1 reshape.12
  24.7 0.4 collective-permute-start.5
  25.1 2.5 %collective-permute-start.6 = (f32[16,128]{1,0:T(8,128)S(1)}, f32[16,128]{1,0:T(8,128)S(1)}, u32[]{:S(2)}, u32[]{:S(2)}) collective-permute-start(f32[16,128]{1,0:T(8,128)S(1)} %get-tuple-element.26), channel_id=1, source_target_pairs={{0,16},{1,17},{2,18},{3,19},{4,20},{5,21},{6,22},{7,23},{8,24},{9,... | collective-permute-start | bytes 24584 | tf_op jit(solution)/shard_map/ppermute | solution.py:440
  27.6 1.3 %collective-permute-start.7 = (f32[16,128]{1,0:T(8,128)S(1)}, f32[16,128]{1,0:T(8,128)S(1)}, u32[]{:S(2)}, u32[]{:S(2)}) collective-permute-start(f32[16,128]{1,0:T(8,128)S(1)} %get-tuple-element.27), channel_id=1, source_target_pairs={{0,20},{1,21},{2,22},{3,23},{4,16},{5,17},{6,18},{7,19},{8,28},{9,... | collective-permute-start | bytes 24584 | tf_op jit(solution)/shard_map/ppermute | solution.py:440
  29.0 3.5 %collective-permute-start.8 = (f32[16,128]{1,0:T(8,128)S(1)}, f32[16,128]{1,0:T(8,128)S(1)}, u32[]{:S(2)}, u32[]{:S(2)}) collective-permute-start(f32[16,128]{1,0:T(8,128)S(1)} %get-tuple-element.28), channel_id=1, source_target_pairs={{0,24},{1,25},{2,26},{3,27},{4,28},{5,29},{6,30},{7,31},{8,16},{9,... | collective-permute-start | bytes 24584 | tf_op jit(solution)/shard_map/ppermute | solution.py:440
  32.5 0.2 collective-permute-start.9
  32.8 0.1 pad_maximum_fusion.refs_8_
  32.8 0.2 collective-permute-done.7.refs_5_
  33.1 1.4 %collective-permute-done.8.refs_6_ = f32[16,128]{1,0:T(8,128)S(1)} collective-permute-done((f32[16,128]{1,0:T(8,128)S(1)}, f32[16,128]{1,0:T(8,128)S(1)}, u32[]{:S(2)}, u32[]{:S(2)}) %collective-permute-start.8) | collective-permute-done | bytes 8224 | tf_op jit(solution)/shard_map/ppermute | solution.py:440
  34.4 4.4 %collective-permute-done.9.refs_7_ = f32[16,128]{1,0:T(8,128)S(1)} collective-permute-done((f32[16,128]{1,0:T(8,128)S(1)}, f32[16,128]{1,0:T(8,128)S(1)}, u32[]{:S(2)}, u32[]{:S(2)}) %collective-permute-start.9) | collective-permute-done | bytes 8224 | tf_op jit(solution)/shard_map/ppermute | solution.py:440
  38.9 0.3 far_sum.1.refs_0_
  39.2 0.2 collective-permute-start.16
  39.4 3.5 %collective-permute-start.15 = (f32[24,128]{1,0:T(8,128)S(1)}, f32[24,128]{1,0:T(8,128)S(1)}, u32[]{:S(2)}, u32[]{:S(2)}) collective-permute-start(f32[24,128]{1,0:T(8,128)S(1)} %far_sum.1.refs_0_), channel_id=1, source_target_pairs={{0,24},{1,25},{2,26},{3,27},{4,28},{5,29},{6,30},{7,31},{8,16},{9,... | collective-permute-start | bytes 36872 | tf_op jit(solution)/shard_map/ppermute | solution.py:440
  43.0 0.0 collective-permute-start.14
  43.0 3.9 %collective-permute-start.13 = (f32[24,128]{1,0:T(8,128)S(1)}, f32[24,128]{1,0:T(8,128)S(1)}, u32[]{:S(2)}, u32[]{:S(2)}) collective-permute-start(f32[24,128]{1,0:T(8,128)S(1)} %far_sum.1.refs_0_), channel_id=1, source_target_pairs={{0,16},{1,17},{2,18},{3,19},{4,20},{5,21},{6,22},{7,23},{8,24},{9,... | collective-permute-start | bytes 36872 | tf_op jit(solution)/shard_map/ppermute | solution.py:440
  46.9 0.0 collective-permute-start.12
  46.9 0.0 collective-permute-done.16.refs_7_
  46.9 2.0 %collective-permute-start.11 = (f32[24,128]{1,0:T(8,128)S(1)}, f32[24,128]{1,0:T(8,128)S(1)}, u32[]{:S(2)}, u32[]{:S(2)}) collective-permute-start(f32[24,128]{1,0:T(8,128)S(1)} %far_sum.1.refs_0_), channel_id=1, source_target_pairs={{0,8},{1,9},{2,10},{3,11},{4,12},{5,13},{6,14},{7,15},{8,0},{9,1},... | collective-permute-start | bytes 36872 | tf_op jit(solution)/shard_map/ppermute | solution.py:440
  48.8 1.5 %collective-permute-start.10 = (f32[24,128]{1,0:T(8,128)S(1)}, f32[24,128]{1,0:T(8,128)S(1)}, u32[]{:S(2)}, u32[]{:S(2)}) collective-permute-start(f32[24,128]{1,0:T(8,128)S(1)} %far_sum.1.refs_0_), channel_id=1, source_target_pairs={{0,4},{1,5},{2,6},{3,7},{4,0},{5,1},{6,2},{7,3},{8,12},{9,13},{10,... | collective-permute-start | bytes 36872 | tf_op jit(solution)/shard_map/ppermute | solution.py:440
  50.4 0.0 collective-permute-done.13.refs_4_
  50.4 1.1 %collective-permute-done.12.refs_3_ = f32[24,128]{1,0:T(8,128)S(1)} collective-permute-done((f32[24,128]{1,0:T(8,128)S(1)}, f32[24,128]{1,0:T(8,128)S(1)}, u32[]{:S(2)}, u32[]{:S(2)}) %collective-permute-start.12) | collective-permute-done | bytes 12320 | tf_op jit(solution)/shard_map/ppermute | solution.py:440
  51.5 1.1 %collective-permute-done.10.refs_1_ = f32[24,128]{1,0:T(8,128)S(1)} collective-permute-done((f32[24,128]{1,0:T(8,128)S(1)}, f32[24,128]{1,0:T(8,128)S(1)}, u32[]{:S(2)}, u32[]{:S(2)}) %collective-permute-start.10) | collective-permute-done | bytes 12320 | tf_op jit(solution)/shard_map/ppermute | solution.py:440
  52.5 0.1 collective-permute-start.20
  52.6 1.3 %collective-permute-start.19 = (f32[8,128]{1,0:T(8,128)S(1)}, f32[8,128]{1,0:T(8,128)S(1)}, u32[]{:S(2)}, u32[]{:S(2)}) collective-permute-start(f32[8,128]{1,0:T(8,128)S(1)} %get-tuple-element.33.refs_4_), channel_id=1, source_target_pairs={{0,1},{1,0},{2,3},{3,2},{4,5},{5,4},{6,7},{7,6},{8,9},{9,8},{10,11... | collective-permute-start | bytes 12296 | tf_op jit(solution)/shard_map/ppermute | solution.py:440
  53.9 0.5 collective-permute-start.18
  54.5 1.2 %collective-permute-done.20.refs_7_ = f32[8,128]{1,0:T(8,128)S(1)} collective-permute-done((f32[8,128]{1,0:T(8,128)S(1)}, f32[8,128]{1,0:T(8,128)S(1)}, u32[]{:S(2)}, u32[]{:S(2)}) %collective-permute-start.20) | collective-permute-done | bytes 4128 | tf_op jit(solution)/shard_map/ppermute | solution.py:440
  55.6 0.7 collective-permute-done.19.refs_6_
  56.3 1.4 %copy-done.1 = bf16[2112,384]{1,0:T(8,128)(2,1)S(1)} copy-done((bf16[2112,384]{1,0:T(8,128)(2,1)S(1)}, bf16[2112,384]{1,0:T(8,128)(2,1)}, u32[]{:S(2)}) %copy-start.1) | copy-done | bytes 1622040
  57.7 1.4 %copy-done.2 = bf16[2112,384]{1,0:T(8,128)(2,1)S(1)} copy-done((bf16[2112,384]{1,0:T(8,128)(2,1)S(1)}, bf16[2112,384]{1,0:T(8,128)(2,1)}, u32[]{:S(2)}) %copy-start.2) | copy-done | bytes 1622040
  59.2 2.1 %local_modes.1.kept_ref = f32[2,6,32,128]{3,2,1,0:T(8,128)S(1)} custom-call(bf16[2112,384]{1,0:T(8,128)(2,1)S(1)} %copy-done.1, bf16[2112,384]{1,0:T(8,128)(2,1)S(1)} %copy-done.2, f32[6,128]{1,0:T(8,128)S(1)} %bitcast.6, f32[2,128,128]{2,1,0:T(8,128)S(1)} %copy-done.3, f32[8,128]{1,0:T(8,128)S(1)} %get-tuple-element.33.refs_4_, ...), custom_call_target="tpu_custom_call" | custom-call | tf_op jit(solution)/shard_map/local_modes/pallas_call | solution.py:397
  61.2 1.3 %collective-permute-start.21 = (f32[6,32,128]{2,1,0:T(8,128)S(1)}, f32[6,32,128]{2,1,0:T(8,128)S(1)}, u32[]{:S(2)}, u32[]{:S(2)}) collective-permute-start(f32[6,32,128]{2,1,0:T(8,128)S(1)} %slice_bitcast_fusion), channel_id=1, source_target_pairs={{0,1},{1,0},{2,3},{3,2},{4,5},{5,4},{6,7},{7,6},{8,9},{9,8},{10,11... | collective-permute-start | bytes 294920 | tf_op jit(solution)/shard_map/ppermute | solution.py:440
  62.6 1.3 %collective-permute-done.17.refs_1_ = f32[8,16,128]{2,1,0:T(8,128)S(1)} collective-permute-done((f32[8,16,128]{2,1,0:T(8,128)S(1)}, f32[8,16,128]{2,1,0:T(8,128)S(1)}, u32[]{:S(2)}, u32[]{:S(2)}) %collective-permute-start.17) | collective-permute-done | bytes 65568 | tf_op jit(solution)/shard_map/ppermute | solution.py:440
  63.8 3.0 %unpack_gram.1 = f32[32,2,32,32]{3,2,1,0:T(8,128)} custom-call(f32[8,16,128]{2,1,0:T(8,128)S(1)} %get-tuple-element.30.refs_0_, f32[8,16,128]{2,1,0:T(8,128)S(1)} %collective-permute-done.17.refs_1_), custom_call_target="tpu_custom_call" | custom-call | tf_op jit(solution)/shard_map/unpack_gram/pallas_call | solution.py:256
  66.8 0.8 %join_modes.1 = f32[32,2,768]{2,1,0:T(2,128)} custom-call(f32[2,6,32,128]{3,2,1,0:T(8,128)S(1)} %local_modes.1.kept_ref, f32[6,32,128]{2,1,0:T(8,128)S(1)} %collective-permute-done.21.got_ref), custom_call_target="tpu_custom_call" | custom-call | tf_op jit(solution)/shard_map/join_modes/pallas_call | solution.py:256
  (20 shorter events, 0.1 us)
Async XLA Ops:
  0.6 23.7 %copy-start = (f32[64,2,32]{0,2,1:T(8,128)S(1)}, f32[64,2,32]{0,2,1:T(8,128)}, u32[]{:S(2)}) copy-start(f32[64,2,32]{0,2,1:T(8,128)} %param.7) | copy-start | bytes 49156
  0.6 55.7 %copy-start.3 = (f32[2,128,128]{2,1,0:T(8,128)S(1)}, f32[2,128,128]{2,1,0:T(8,128)}, u32[]{:S(2)}) copy-start(f32[2,128,128]{2,1,0:T(8,128)} %constant.26.clone.refs_3_) | copy-start | bytes 393220
  0.7 55.6 %copy-start.5 = (f32[768]{0:T(1024)S(1)}, f32[768]{0:T(1024)}, u32[]{:S(2)}) copy-start(f32[768]{0:T(1024)} %param.6) | copy-start | bytes 9220
  12.9 3.2 %collective-permute-start = (f32[8,16,128]{2,1,0:T(8,128)}, f32[8,16,128]{2,1,0:T(8,128)S(1)}, u32[]{:S(2)}, u32[]{:S(2)}) collective-permute-start(f32[8,16,128]{2,1,0:T(8,128)} %get-tuple-element.19), channel_id=1, source_target_pairs={{0,2},{1,3},{2,0},{3,1},{4,6},{5,7},{6,4},{7,5},{8,10},{9,11},{10,... | collective-permute-start | bytes 196616 | tf_op jit(solution)/shard_map/ppermute | solution.py:440
  13.4 5.5 %collective-permute-start.1 = (f32[8,16,128]{2,1,0:T(8,128)}, f32[8,16,128]{2,1,0:T(8,128)S(1)}, u32[]{:S(2)}, u32[]{:S(2)}) collective-permute-start(f32[8,16,128]{2,1,0:T(8,128)} %get-tuple-element.20), channel_id=1, source_target_pairs={{0,1},{1,0},{2,3},{3,2},{4,5},{5,4},{6,7},{7,6},{8,9},{9,8},{10,11... | collective-permute-start | bytes 196616 | tf_op jit(solution)/shard_map/ppermute | solution.py:440
  16.0 4.3 %collective-permute-start.2 = (f32[8,16,128]{2,1,0:T(8,128)}, f32[8,16,128]{2,1,0:T(8,128)S(1)}, u32[]{:S(2)}, u32[]{:S(2)}) collective-permute-start(f32[8,16,128]{2,1,0:T(8,128)} %get-tuple-element.21), channel_id=1, source_target_pairs={{0,3},{1,2},{2,1},{3,0},{4,7},{5,6},{6,5},{7,4},{8,11},{9,10},{10,... | collective-permute-start | bytes 196616 | tf_op jit(solution)/shard_map/ppermute | solution.py:440
  20.3 0.8 %copy-start.4 = (f32[8,16,128]{2,1,0:T(8,128)S(1)}, f32[8,16,128]{2,1,0:T(8,128)}, u32[]{:S(2)}) copy-start(f32[8,16,128]{2,1,0:T(8,128)} %get-tuple-element.18.refs_0_) | copy-start | bytes 196612
  21.2 7.8 %collective-permute-start.3 = (f32[16,128]{1,0:T(8,128)S(1)}, f32[16,128]{1,0:T(8,128)S(1)}, u32[]{:S(2)}, u32[]{:S(2)}) collective-permute-start(f32[16,128]{1,0:T(8,128)S(1)} %get-tuple-element.23), channel_id=1, source_target_pairs={{0,4},{1,5},{2,6},{3,7},{4,0},{5,1},{6,2},{7,3},{8,12},{9,13},{10,... | collective-permute-start | bytes 24584 | tf_op jit(solution)/shard_map/ppermute | solution.py:440
  22.8 9.8 %collective-permute-start.4 = (f32[16,128]{1,0:T(8,128)S(1)}, f32[16,128]{1,0:T(8,128)S(1)}, u32[]{:S(2)}, u32[]{:S(2)}) collective-permute-start(f32[16,128]{1,0:T(8,128)S(1)} %get-tuple-element.24), channel_id=1, source_target_pairs={{0,8},{1,9},{2,10},{3,11},{4,12},{5,13},{6,14},{7,15},{8,0},{9,1},... | collective-permute-start | bytes 24584 | tf_op jit(solution)/shard_map/ppermute | solution.py:440
  24.7 8.2 %collective-permute-start.5 = (f32[16,128]{1,0:T(8,128)S(1)}, f32[16,128]{1,0:T(8,128)S(1)}, u32[]{:S(2)}, u32[]{:S(2)}) collective-permute-start(f32[16,128]{1,0:T(8,128)S(1)} %get-tuple-element.25), channel_id=1, source_target_pairs={{0,12},{1,13},{2,14},{3,15},{4,8},{5,9},{6,10},{7,11},{8,4},{9,5},... | collective-permute-start | bytes 24584 | tf_op jit(solution)/shard_map/ppermute | solution.py:440
  25.1 7.7 %collective-permute-start.6 = (f32[16,128]{1,0:T(8,128)S(1)}, f32[16,128]{1,0:T(8,128)S(1)}, u32[]{:S(2)}, u32[]{:S(2)}) collective-permute-start(f32[16,128]{1,0:T(8,128)S(1)} %get-tuple-element.26), channel_id=1, source_target_pairs={{0,16},{1,17},{2,18},{3,19},{4,20},{5,21},{6,22},{7,23},{8,24},{9,... | collective-permute-start | bytes 24584 | tf_op jit(solution)/shard_map/ppermute | solution.py:440
  27.6 5.4 %collective-permute-start.7 = (f32[16,128]{1,0:T(8,128)S(1)}, f32[16,128]{1,0:T(8,128)S(1)}, u32[]{:S(2)}, u32[]{:S(2)}) collective-permute-start(f32[16,128]{1,0:T(8,128)S(1)} %get-tuple-element.27), channel_id=1, source_target_pairs={{0,20},{1,21},{2,22},{3,23},{4,16},{5,17},{6,18},{7,19},{8,28},{9,... | collective-permute-start | bytes 24584 | tf_op jit(solution)/shard_map/ppermute | solution.py:440
  29.0 5.4 %collective-permute-start.8 = (f32[16,128]{1,0:T(8,128)S(1)}, f32[16,128]{1,0:T(8,128)S(1)}, u32[]{:S(2)}, u32[]{:S(2)}) collective-permute-start(f32[16,128]{1,0:T(8,128)S(1)} %get-tuple-element.28), channel_id=1, source_target_pairs={{0,24},{1,25},{2,26},{3,27},{4,28},{5,29},{6,30},{7,31},{8,16},{9,... | collective-permute-start | bytes 24584 | tf_op jit(solution)/shard_map/ppermute | solution.py:440
  32.5 6.3 %collective-permute-start.9 = (f32[16,128]{1,0:T(8,128)S(1)}, f32[16,128]{1,0:T(8,128)S(1)}, u32[]{:S(2)}, u32[]{:S(2)}) collective-permute-start(f32[16,128]{1,0:T(8,128)S(1)} %get-tuple-element.29), channel_id=1, source_target_pairs={{0,28},{1,29},{2,30},{3,31},{4,24},{5,25},{6,26},{7,27},{8,20},{9,... | collective-permute-start | bytes 24584 | tf_op jit(solution)/shard_map/ppermute | solution.py:440
  39.2 7.7 %collective-permute-start.16 = (f32[24,128]{1,0:T(8,128)S(1)}, f32[24,128]{1,0:T(8,128)S(1)}, u32[]{:S(2)}, u32[]{:S(2)}) collective-permute-start(f32[24,128]{1,0:T(8,128)S(1)} %far_sum.1.refs_0_), channel_id=1, source_target_pairs={{0,28},{1,29},{2,30},{3,31},{4,24},{5,25},{6,26},{7,27},{8,20},{9,... | collective-permute-start | bytes 36872 | tf_op jit(solution)/shard_map/ppermute | solution.py:440
  39.4 9.4 %collective-permute-start.15 = (f32[24,128]{1,0:T(8,128)S(1)}, f32[24,128]{1,0:T(8,128)S(1)}, u32[]{:S(2)}, u32[]{:S(2)}) collective-permute-start(f32[24,128]{1,0:T(8,128)S(1)} %far_sum.1.refs_0_), channel_id=1, source_target_pairs={{0,24},{1,25},{2,26},{3,27},{4,28},{5,29},{6,30},{7,31},{8,16},{9,... | collective-permute-start | bytes 36872 | tf_op jit(solution)/shard_map/ppermute | solution.py:440
  43.0 7.4 %collective-permute-start.14 = (f32[24,128]{1,0:T(8,128)S(1)}, f32[24,128]{1,0:T(8,128)S(1)}, u32[]{:S(2)}, u32[]{:S(2)}) collective-permute-start(f32[24,128]{1,0:T(8,128)S(1)} %far_sum.1.refs_0_), channel_id=1, source_target_pairs={{0,20},{1,21},{2,22},{3,23},{4,16},{5,17},{6,18},{7,19},{8,28},{9,... | collective-permute-start | bytes 36872 | tf_op jit(solution)/shard_map/ppermute | solution.py:440
  43.0 7.4 %collective-permute-start.13 = (f32[24,128]{1,0:T(8,128)S(1)}, f32[24,128]{1,0:T(8,128)S(1)}, u32[]{:S(2)}, u32[]{:S(2)}) collective-permute-start(f32[24,128]{1,0:T(8,128)S(1)} %far_sum.1.refs_0_), channel_id=1, source_target_pairs={{0,16},{1,17},{2,18},{3,19},{4,20},{5,21},{6,22},{7,23},{8,24},{9,... | collective-permute-start | bytes 36872 | tf_op jit(solution)/shard_map/ppermute | solution.py:440
  46.9 4.6 %collective-permute-start.12 = (f32[24,128]{1,0:T(8,128)S(1)}, f32[24,128]{1,0:T(8,128)S(1)}, u32[]{:S(2)}, u32[]{:S(2)}) collective-permute-start(f32[24,128]{1,0:T(8,128)S(1)} %far_sum.1.refs_0_), channel_id=1, source_target_pairs={{0,12},{1,13},{2,14},{3,15},{4,8},{5,9},{6,10},{7,11},{8,4},{9,5},... | collective-permute-start | bytes 36872 | tf_op jit(solution)/shard_map/ppermute | solution.py:440
  46.9 4.6 %collective-permute-start.11 = (f32[24,128]{1,0:T(8,128)S(1)}, f32[24,128]{1,0:T(8,128)S(1)}, u32[]{:S(2)}, u32[]{:S(2)}) collective-permute-start(f32[24,128]{1,0:T(8,128)S(1)} %far_sum.1.refs_0_), channel_id=1, source_target_pairs={{0,8},{1,9},{2,10},{3,11},{4,12},{5,13},{6,14},{7,15},{8,0},{9,1},... | collective-permute-start | bytes 36872 | tf_op jit(solution)/shard_map/ppermute | solution.py:440
  48.8 3.7 %collective-permute-start.10 = (f32[24,128]{1,0:T(8,128)S(1)}, f32[24,128]{1,0:T(8,128)S(1)}, u32[]{:S(2)}, u32[]{:S(2)}) collective-permute-start(f32[24,128]{1,0:T(8,128)S(1)} %far_sum.1.refs_0_), channel_id=1, source_target_pairs={{0,4},{1,5},{2,6},{3,7},{4,0},{5,1},{6,2},{7,3},{8,12},{9,13},{10,... | collective-permute-start | bytes 36872 | tf_op jit(solution)/shard_map/ppermute | solution.py:440
  52.5 3.1 %collective-permute-start.20 = (f32[8,128]{1,0:T(8,128)S(1)}, f32[8,128]{1,0:T(8,128)S(1)}, u32[]{:S(2)}, u32[]{:S(2)}) collective-permute-start(f32[8,128]{1,0:T(8,128)S(1)} %get-tuple-element.33.refs_4_), channel_id=1, source_target_pairs={{0,3},{1,2},{2,1},{3,0},{4,7},{5,6},{6,5},{7,4},{8,11},{9,10},{10,... | collective-permute-start | bytes 12296 | tf_op jit(solution)/shard_map/ppermute | solution.py:440
  52.6 3.7 %collective-permute-start.19 = (f32[8,128]{1,0:T(8,128)S(1)}, f32[8,128]{1,0:T(8,128)S(1)}, u32[]{:S(2)}, u32[]{:S(2)}) collective-permute-start(f32[8,128]{1,0:T(8,128)S(1)} %get-tuple-element.33.refs_4_), channel_id=1, source_target_pairs={{0,1},{1,0},{2,3},{3,2},{4,5},{5,4},{6,7},{7,6},{8,9},{9,8},{10,11... | collective-permute-start | bytes 12296 | tf_op jit(solution)/shard_map/ppermute | solution.py:440
  53.9 2.4 %collective-permute-start.18 = (f32[8,128]{1,0:T(8,128)S(1)}, f32[8,128]{1,0:T(8,128)S(1)}, u32[]{:S(2)}, u32[]{:S(2)}) collective-permute-start(f32[8,128]{1,0:T(8,128)S(1)} %get-tuple-element.33.refs_4_), channel_id=1, source_target_pairs={{0,2},{1,3},{2,0},{3,1},{4,6},{5,7},{6,4},{7,5},{8,10},{9,11},{10,... | collective-permute-start | bytes 12296 | tf_op jit(solution)/shard_map/ppermute | solution.py:440
  56.3 1.4 %copy-start.1 = (bf16[2112,384]{1,0:T(8,128)(2,1)S(1)}, bf16[2112,384]{1,0:T(8,128)(2,1)}, u32[]{:S(2)}) copy-start(bf16[2112,384]{1,0:T(8,128)(2,1)} %get-tuple-element.31.refs_0_) | copy-start | bytes 4866052
  57.7 1.4 %copy-start.2 = (bf16[2112,384]{1,0:T(8,128)(2,1)S(1)}, bf16[2112,384]{1,0:T(8,128)(2,1)}, u32[]{:S(2)}) copy-start(bf16[2112,384]{1,0:T(8,128)(2,1)} %get-tuple-element.32.refs_1_) | copy-start | bytes 4866052
  61.2 5.5 %collective-permute-start.21 = (f32[6,32,128]{2,1,0:T(8,128)S(1)}, f32[6,32,128]{2,1,0:T(8,128)S(1)}, u32[]{:S(2)}, u32[]{:S(2)}) collective-permute-start(f32[6,32,128]{2,1,0:T(8,128)S(1)} %slice_bitcast_fusion), channel_id=1, source_target_pairs={{0,1},{1,0},{2,3},{3,2},{4,5},{5,4},{6,7},{7,6},{8,9},{9,8},{10,11... | collective-permute-start | bytes 294920 | tf_op jit(solution)/shard_map/ppermute | solution.py:440
  62.6 1.3 %collective-permute-start.17 = (f32[8,16,128]{2,1,0:T(8,128)S(1)}, f32[8,16,128]{2,1,0:T(8,128)S(1)}, u32[]{:S(2)}, u32[]{:S(2)}) collective-permute-start(f32[8,16,128]{2,1,0:T(8,128)S(1)} %get-tuple-element.30.refs_0_), channel_id=1, source_target_pairs={{0,2},{1,3},{2,0},{3,1},{4,6},{5,7},{6,4},{7,5},{8,10},{9,11},{10,... | collective-permute-start | bytes 196616 | tf_op jit(solution)/shard_map/ppermute | solution.py:440
where the time goes:
time: 67.8 us; the launch traced here: 67.6 us
  starting transfers between devices  28.8 us (42%)
  Pallas kernels  18.4 us (27%)
  waiting for transfers between devices  15.6 us (23%)
  local copies, waits for them, and re-layouts  4.01 us (6%)
  between operations  0.75 us (1%)
    ppermute x22, starting transfers between devices, swap(): lax.ppermute(value, ('pts', 'freq'), [(i, i ^ mask) for i in range(n_devi...  28.8 us
    ppermute x22, waiting for transfers between devices, swap(): lax.ppermute(value, ('pts', 'freq'), [(i, i ^ mask) for i in range(n_devi...  15.6 us
    pallas_call x1, Pallas kernels, gram_parts(): pl.pallas_call(functools.partial(gram_kernel, total_rows, chunks), out_sh...  12.2 us
    pallas_call x5, Pallas kernels, call(): pl.pallas_call(kernel, out_shape=out_shape, in_specs=[VMEM] * len(args),...  4.13 us
    unnamed x12, local copies, waits for them, and re-layouts  3.7 us
    pallas_call x1, Pallas kernels, local_modes(): pl.pallas_call(functools.partial(modes_kernel, total_rows, n_resp), out_s...  2.05 us
  transfers between devices with their start and end apart: 22, of which 10 were waited for; matrix products, arithmetic and copies ran while one was open for 1% of the time, Pallas kernels for 4%

commit v1 on v0

v1 whole, which is shorter than its diff:
```python
import functools
import math

import jax
import jax.numpy as jnp
import numpy as np
from jax import lax
from jax.experimental import pallas as pl
from jax.experimental.pallas import tpu as pltpu
from jax.sharding import PartitionSpec as P

NFFT = 128
HALF = NFFT // 2
NF = 64
NB = 32
LANES = 128
PACK = 4
VMEM_LIMIT = 56 * 1024 * 1024
SMALL_LIMIT = 16 * 1024 * 1024
VMEM = pl.BlockSpec(memory_space=pltpu.VMEM)


def dft_values():
    times = np.arange(NFFT)
    freqs = np.arange(NF)
    phases = (freqs[:, None] * times[None, :] % NFFT) * (2.0 * math.pi / NFFT)
    window = 0.5 - 0.5 * np.cos(times * (2.0 * math.pi / NFFT))
    weighted = window / np.sqrt(np.sum(window * window))
    return np.cos(phases) * weighted, -np.sin(phases) * weighted


def split_table(table):
    high = table.astype(jnp.bfloat16)
    low = (table - high.astype(np.float64)).astype(jnp.bfloat16)
    return high, low


def dft_operand():
    real, imag = dft_values()
    high, low = split_table(np.concatenate([real, imag], axis=0))
    return np.block([[high, high], [low, np.zeros_like(low)]])


def mode_tables():
    real, imag = dft_values()
    order = np.concatenate([np.arange(0, NF, 2), np.arange(1, NF, 2)])
    real, imag = real[order].T, imag[order].T
    first = np.concatenate([real, imag], axis=1)
    second = np.concatenate([-imag, real], axis=1)
    return np.stack([first, second]).astype(np.float32)


def split(value):
    high = value.astype(jnp.bfloat16)
    low = (value - high.astype(jnp.float32)).astype(jnp.bfloat16)
    return high, low


def load_weights(w_ref, col_tiles):
    first = lax.axis_index("freq") * col_tiles
    return jnp.concatenate([w_ref[pl.ds(first + c, 1), :] for c in range(col_tiles)], axis=1)


def flip_groups(groups, flipped):
    turned = flipped.T
    lane = lax.broadcasted_iota(jnp.int32, (NB, LANES), 1)
    out = []
    for g in range(PACK):
        total = groups[g]
        for q in range(PACK):
            block = turned[q * NB : (q + 1) * NB]
            if q != g:
                block = pltpu.roll(block, ((q - g) % PACK) * NB, 1)
            total = total + jnp.where(lane // NB == q, block, 0.0)
        out.append(total)
    return out


ROW_STEP = 3
FREQ_STEP = ROW_STEP * NB + 1


def gram_kernel(
    total_rows,
    places,
    x_hbm,
    w_hbm,
    dft_hbm,
    out_ref,
    high_hbm,
    low_hbm,
    x_ref,
    w_ref,
    dft_ref,
    high_ref,
    low_ref,
    spec_ref,
    z_even,
    z_odd,
    direct_ref,
    flipped_ref,
    in_sems,
    out_sems,
):
    times, cols = x_ref.shape
    halves = times // HALF
    col_tiles = cols // LANES
    pieces = in_sems.shape[0] - 2
    piece = times // pieces

    def fetch(i):
        rows = pl.ds(i * piece, piece)
        return pltpu.make_async_copy(x_hbm.at[rows], x_ref.at[rows], in_sems.at[i])

    fetch_w = pltpu.make_async_copy(w_hbm, w_ref, in_sems.at[pieces])
    fetch_dft = pltpu.make_async_copy(dft_hbm, dft_ref, in_sems.at[pieces + 1])
    for i in range(pieces):
        fetch(i).start()
    fetch_w.start()
    fetch_dft.start()

    acc = jnp.zeros((HALF, cols), jnp.float32)
    for i in range(pieces):
        fetch(i).wait()
        for h in range(piece // HALF):
            acc = acc + x_ref[pl.ds(i * piece + h * HALF, HALF), :]
    mean = jnp.sum(acc, axis=0, keepdims=True) / times
    fetch_w.wait()
    scale = jnp.sqrt(load_weights(w_ref, col_tiles) / (2.0 * total_rows))

    def center(i, carry):
        rows = pl.ds(pl.multiple_of(i * HALF, HALF), HALF)
        high, low = split((x_ref[rows, :] - mean) * scale)
        high_ref[rows, :] = high
        low_ref[rows, :] = low
        return carry

    lax.fori_loop(0, halves, center, 0, unroll=3)
    save_high = pltpu.make_async_copy(high_ref, high_hbm, out_sems.at[0])
    save_low = pltpu.make_async_copy(low_ref, low_hbm, out_sems.at[1])
    save_high.start()
    save_low.start()
    fetch_dft.wait()

    def transform(i, carry):
        blocks = []
        for s in range(2):
            rows = pl.ds(pl.multiple_of((2 * i + s) * HALF, HALF), NFFT)
            blocks.append(jnp.concatenate([high_ref[rows, :], low_ref[rows, :]], axis=0))
        both = jnp.dot(
            dft_ref[...], jnp.concatenate(blocks, axis=1), preferred_element_type=jnp.float32
        )
        spectrum = both[: 2 * NF] + both[2 * NF :]
        for s in range(2):
            for o in range(2 * NF // 8):
                for c in range(col_tiles):
                    first = s * cols + c * LANES
                    rows = pl.ds(ROW_STEP * (2 * i + s), 8, stride=FREQ_STEP)
                    spec_ref[c, o, rows, :] = spectrum[8 * o : 8 * o + 8, first : first + LANES]
        return carry

    lax.fori_loop(0, NB // 2, transform, 0, unroll=2)

    row = lax.broadcasted_iota(jnp.int32, (NB, LANES), 0)
    lane = lax.broadcasted_iota(jnp.int32, (NB, LANES), 1)
    upper = row <= lane % NB
    lower = row >= lane % NB
    octets = NF // 8

    def prepare(z_ref, octet, half):
        for part in range(2):
            for q in range(PACK):
                rows = pl.ds(FREQ_STEP * (PACK * half + q), NB, stride=ROW_STEP)
                own = pl.ds(part * LANES + q * NB, NB)
                for c in range(col_tiles):
                    value = spec_ref[c, octet + octets * part, rows, :]
                    high = value.astype(jnp.bfloat16)
                    low = (2.0 * (value - high.astype(jnp.float32))).astype(jnp.bfloat16)
                    z_ref[own, pl.ds(c * LANES, LANES)] = high
                    z_ref[own, pl.ds(cols + c * LANES, LANES)] = low

    def correlate(z_ref, group):
        high = z_ref[:, pl.ds(0, cols)]
        product = lax.dot_general(
            jnp.concatenate([high, high], axis=1),
            z_ref[...],
            (((1,), (1,)), ((), ())),
            preferred_element_type=jnp.float32,
        )
        gram_real = jnp.zeros((NB, LANES), jnp.float32)
        gram_imag = jnp.zeros((NB, LANES), jnp.float32)
        for q in range(PACK):
            mine = lane // NB == q
            real = product[q * NB : (q + 1) * NB]
            imag = product[LANES + q * NB : LANES + (q + 1) * NB]
            gram_real = jnp.where(mine, real[:, :LANES] + imag[:, LANES:], gram_real)
            gram_imag = jnp.where(mine, real[:, LANES:] - imag[:, :LANES], gram_imag)
        direct_ref[group] = jnp.where(upper, gram_real, gram_imag)
        flipped_ref[group] = jnp.where(lower, gram_real, -gram_imag)

    prepare(z_even, 0, 0)

    def step(o, carry):
        prepare(z_odd, o, 1)
        correlate(z_even, 2 * o)
        prepare(z_even, jnp.minimum(o + 1, octets - 1), 0)
        correlate(z_odd, 2 * o + 1)
        return carry

    lax.fori_loop(0, octets, step, 0)
    left = lane[: NB // 2] < LANES // 2
    for quad in range(NF // PACK // PACK):
        groups = [direct_ref[quad * PACK + g] for g in range(PACK)]
        flipped = flipped_ref[pl.ds(quad * PACK, PACK)].reshape(PACK * NB, LANES)
        for g, packed in enumerate(flip_groups(groups, flipped)):
            top = packed[: NB // 2]
            bottom = packed[NB // 2 :]
            pair = 2 * (quad * PACK + g)
            out_ref[places[pair]] = jnp.where(left, top, pltpu.roll(bottom, LANES // 2, 1))
            out_ref[places[pair + 1]] = jnp.where(left, pltpu.roll(top, LANES // 2, 1), bottom)
    save_high.wait()
    save_low.wait()


def gram_parts(snapshots, weight_rows, total_rows, places):
    times, cols = snapshots.shape
    dft = dft_operand()
    pieces = 11
    any_space = pl.BlockSpec(memory_space=pl.ANY)
    saved = jax.ShapeDtypeStruct((times, cols), jnp.bfloat16)
    return pl.pallas_call(
        functools.partial(gram_kernel, total_rows, places),
        out_shape=(jax.ShapeDtypeStruct((NF // 2, NB // 2, LANES), jnp.float32), saved, saved),
        in_specs=[any_space] * 3,
        out_specs=(VMEM, any_space, any_space),
        scratch_shapes=[
            pltpu.VMEM((times, cols), jnp.float32),
            pltpu.VMEM(weight_rows.shape, jnp.float32),
            pltpu.VMEM(dft.shape, jnp.bfloat16),
            pltpu.VMEM((times, cols), jnp.bfloat16),
            pltpu.VMEM((times, cols), jnp.bfloat16),
            pltpu.VMEM((cols // LANES, 2 * NF // 8, 8 * FREQ_STEP, LANES), jnp.float32),
            pltpu.VMEM((2 * LANES, 2 * cols), jnp.bfloat16),
            pltpu.VMEM((2 * LANES, 2 * cols), jnp.bfloat16),
            pltpu.VMEM((NF // PACK, NB, LANES), jnp.float32),
            pltpu.VMEM((NF // PACK, NB, LANES), jnp.float32),
            pltpu.SemaphoreType.DMA((pieces + 2,)),
            pltpu.SemaphoreType.DMA((2,)),
        ],
        compiler_params=pltpu.CompilerParams(vmem_limit_bytes=VMEM_LIMIT),
        cost_estimate=pl.CostEstimate(
            flops=5_000_000_000, bytes_accessed=8_000_000, transcendentals=0
        ),
        name="gram_parts",
    )(snapshots, weight_rows, jnp.asarray(dft))


def hermitian_pair(packed):
    square = jnp.concatenate([packed, pltpu.roll(packed, LANES // 2, 1)], axis=0)
    tall = jnp.concatenate([square] * (LANES // NB), axis=0).T
    row = lax.broadcasted_iota(jnp.int32, (NB, LANES), 0)
    lane = lax.broadcasted_iota(jnp.int32, (NB, LANES), 1)
    flipped = jnp.where(lane // NB == 0, tall[:NB], tall[NB : 2 * NB])
    col = lane % NB
    real = jnp.where(row <= col, square, flipped)
    imag = jnp.where(row > col, square, jnp.where(row < col, -flipped, 0.0))
    return real, imag, lane


def small_call(kernel, name, out_shape, scratch_shapes=(), limit=SMALL_LIMIT):
    def call(*args):
        return pl.pallas_call(
            kernel,
            out_shape=out_shape,
            in_specs=[VMEM] * len(args),
            out_specs=VMEM if isinstance(out_shape, jax.ShapeDtypeStruct) else (VMEM,) * len(out_shape),
            scratch_shapes=list(scratch_shapes),
            compiler_params=pltpu.CompilerParams(vmem_limit_bytes=limit),
            name=name,
        )(*args)

    return call


def floats(*shape):
    return jax.ShapeDtypeStruct(shape, jnp.float32)


def near_sum_kernel(parts_ref, out_ref):
    out_ref[...] = (parts_ref[0] + parts_ref[1]) + (parts_ref[2] + parts_ref[3])


def far_sum_kernel(parts_ref, start_ref, out_ref):
    packed = jnp.sum(parts_ref[...], axis=0)
    real, imag, lane = hermitian_pair(packed)
    start_real = start_ref[0]
    start_imag = start_ref[1]
    resp_real = jnp.sum(real * start_real + imag * start_imag, axis=0, keepdims=True)
    resp_imag = jnp.sum(real * start_imag - imag * start_real, axis=0, keepdims=True)
    power = resp_real * resp_real + resp_imag * resp_imag
    lane = lane[:1]
    first = jnp.sum(jnp.where(lane < NB, power, 0.0), axis=1, keepdims=True) / NB
    second = (
        jnp.sum(jnp.where((lane >= NB) & (lane < 2 * NB), power, 0.0), axis=1, keepdims=True) / NB
    )
    scaling = 1.0 / jnp.sqrt(jnp.where(lane < NB, first, second) + 1e-06)
    resp = jnp.where(
        lane < LANES // 2, resp_real * scaling, pltpu.roll(resp_imag * scaling, LANES // 2, 1)
    )
    resp = jnp.broadcast_to(resp, (8, LANES))
    for n in range(out_ref.shape[0]):
        out_ref[n, pl.ds(0, NB // 2), :] = packed
        out_ref[n, pl.ds(NB // 2, 8), :] = resp


def far_join_kernel(parts_ref, resp_ref, packed_ref):
    for n in range(parts_ref.shape[0]):
        row = parts_ref[n, pl.ds(NB // 2, 1), :]
        for m in range(resp_ref.shape[0]):
            resp_ref[m, pl.ds(n, 1), :] = row
        packed_ref[n] = parts_ref[n, pl.ds(0, NB // 2), :]


def unpack_kernel(*refs):
    parts, out_ref = refs[:-1], refs[-1]
    own = lax.rem(lax.axis_index("pts"), 2)
    row = lax.broadcasted_iota(jnp.int32, (NB, LANES), 0)
    lane = lax.broadcasted_iota(jnp.int32, (NB, LANES), 1)
    left = lane[: NB // 2] < LANES // 2
    col = lane % NB
    zero = jnp.zeros((NB, LANES), jnp.float32)
    for m, part in enumerate(parts):
        count = part.shape[0]
        place = (own ^ m) * 2 * count if len(parts) > 1 else 0
        for first in range(0, count, 2 * PACK):
            squares = []
            for i in range(first, min(first + 2 * PACK, count), 2):
                even, odd = part[i], part[i + 1]
                top = jnp.where(left, even, pltpu.roll(odd, LANES // 2, 1))
                bottom = jnp.where(left, pltpu.roll(even, LANES // 2, 1), odd)
                squares.append(jnp.concatenate([top, bottom], axis=0))
            full = squares + [zero] * (PACK - len(squares))
            turned = flip_groups([zero] * PACK, jnp.concatenate(full, axis=0))
            for g, square in enumerate(squares):
                real = jnp.where(row <= col, square, turned[g])
                imag = jnp.where(row > col, square, jnp.where(row < col, -turned[g], 0.0))
                for q in range(PACK):
                    freq = place + 2 * first + PACK * g + q
                    out_ref[freq, 0] = real[:, q * NB : (q + 1) * NB]
                    out_ref[freq, 1] = imag[:, q * NB : (q + 1) * NB]


def unpack_gram(*parts):
    pairs = sum(part.shape[0] for part in parts)
    return small_call(unpack_kernel, "unpack_gram", floats(2 * pairs, 2, NB, NB))(*parts)


def modes_kernel(
    total_rows, starts, high_hbm, low_hbm, w_hbm, table_hbm, resp_hbm,
    out_ref, resp_ref, w_ref, table_ref, resp_t, a_ref, x_ref, sems,
):
    times, cols = high_hbm.shape
    padded = x_ref.shape[1]
    pairs = NF // 2
    count = pairs // len(starts)
    fetch_resp = [
        pltpu.make_async_copy(
            resp_hbm.at[m], resp_ref.at[pl.ds(start, count)], sems.at[4 + m]
        )
        for m, start in enumerate(starts)
    ]
    fetches = [
        pltpu.make_async_copy(table_hbm, table_ref, sems.at[0]),
        pltpu.make_async_copy(w_hbm, w_ref, sems.at[1]),
        pltpu.make_async_copy(high_hbm, x_ref.at[0, pl.ds(0, times)], sems.at[2]),
        pltpu.make_async_copy(low_hbm, x_ref.at[1, pl.ds(0, times)], sems.at[3]),
    ]
    for fetch in fetch_resp + fetches:
        fetch.start()
    if padded > times:
        pad = pl.ds(times, padded - times)
        x_ref[0, pad, :] = jnp.zeros((padded - times, cols), jnp.bfloat16)
        x_ref[1, pad, :] = jnp.zeros((padded - times, cols), jnp.bfloat16)
    for fetch in fetch_resp + fetches[:2]:
        fetch.wait()
    tall = jnp.concatenate([resp_ref[...]] * (LANES // pairs), axis=0).T
    lane = lax.broadcasted_iota(jnp.int32, (NB, LANES), 1)
    turned = tall[:NB]
    for q in range(1, PACK):
        turned = jnp.where(lane // pairs == q, tall[q * NB : (q + 1) * NB], turned)
    swapped = pltpu.roll(turned, LANES // 2, 1)
    left = lane < LANES // 2
    resp_t[0] = jnp.where(left, turned, swapped)
    resp_t[1] = jnp.where(left, swapped, turned)
    for j in range(padded // HALF):
        value = jnp.zeros((HALF, LANES), jnp.float32)
        for block, start in ((j, 0), (j - 1, HALF)):
            if 0 <= block < NB:
                for part in range(2):
                    value += resp_t[part, pl.ds(block, 1), :] * table_ref[part, pl.ds(start, HALF), :]
        high, low = split(value)
        a_ref[0, pl.ds(j * HALF, HALF), :] = high
        a_ref[1, pl.ds(j * HALF, HALF), :] = low
    dot = functools.partial(
        lax.dot_general,
        dimension_numbers=(((0,), (0,)), ((), ())),
        preferred_element_type=jnp.float32,
    )
    for fetch in fetches[2:]:
        fetch.wait()
    modes = dot(a_ref[0], x_ref[0]) + dot(a_ref[0], x_ref[1]) + dot(a_ref[1], x_ref[0])
    modes = modes * jnp.sqrt(2.0 * total_rows / load_weights(w_ref, cols // LANES))
    n_freq = out_ref.shape[0]
    mine = pairs // n_freq
    group = lax.axis_index("freq")
    for part in range(2):
        for parity in range(2):
            for f in range(n_freq):
                first = (2 * part + parity) * pairs + f * mine
                slot = f ^ group if n_freq == 2 else f
                for c in range(cols // LANES):
                    out_ref[slot, 2 * c + part, pl.ds(parity, mine, stride=2), :] = modes[
                        first : first + mine, c * LANES : (c + 1) * LANES
                    ]


def local_modes(high, low, weight_rows, response, starts, total_rows, n_freq):
    times, cols = high.shape
    padded = -(-times // 256) * 256
    tables = mode_tables()
    any_space = pl.BlockSpec(memory_space=pl.ANY)
    return pl.pallas_call(
        functools.partial(modes_kernel, total_rows, starts),
        out_shape=floats(n_freq, 2 * cols // LANES, NF // n_freq, LANES),
        in_specs=[any_space] * 5,
        out_specs=VMEM,
        scratch_shapes=[
            pltpu.VMEM((NF // 2, LANES), jnp.float32),
            pltpu.VMEM(weight_rows.shape, jnp.float32),
            pltpu.VMEM(tables.shape, jnp.float32),
            pltpu.VMEM((2, NB, LANES), jnp.float32),
            pltpu.VMEM((2, padded, LANES), jnp.bfloat16),
            pltpu.VMEM((2, padded, cols), jnp.bfloat16),
            pltpu.SemaphoreType.DMA((4 + len(starts),)),
        ],
        compiler_params=pltpu.CompilerParams(vmem_limit_bytes=VMEM_LIMIT),
        name="local_modes",
    )(high, low, weight_rows, jnp.asarray(tables), response)


def join_kernel(kept_ref, got_ref, out_ref):
    tiles = got_ref.shape[0] // 2
    group = lax.axis_index("freq")
    for slot, ref in enumerate((kept_ref.at[0], got_ref)):
        for c in range(tiles):
            lanes = pl.ds(pl.multiple_of(((group ^ slot) * tiles + c) * LANES, LANES), LANES)
            for part in range(2):
                out_ref[:, part, lanes] = ref[2 * c + part]


def join_modes(kept, got):
    tiles, count, _ = got.shape
    return small_call(join_kernel, "join_modes", floats(count, 2, tiles * LANES))(kept, got)


def response_of(gram, start_vec):
    matvec = functools.partial(jnp.einsum, "fjk,fk->fj", precision=lax.Precision.HIGHEST)
    resp_real = matvec(gram[:, 0], start_vec[:, 0]) - matvec(gram[:, 1], start_vec[:, 1])
    resp_imag = matvec(gram[:, 0], start_vec[:, 1]) + matvec(gram[:, 1], start_vec[:, 0])
    scaling = 1.0 / jnp.sqrt(
        jnp.mean(resp_real * resp_real + resp_imag * resp_imag, axis=1, keepdims=True) + 1e-06
    )
    return jnp.stack([resp_real * scaling, resp_imag * scaling], axis=1)


def two_level_shards(n_devices, snapshots, weight, start_vec):
    both = ("pts", "freq")
    near = [[4 * i + j for j in range(4)] for i in range(n_devices // 4)]
    far = [[i + 4 * j for j in range(n_devices // 4)] for i in range(4)]
    exchange = functools.partial(
        lax.all_to_all, axis_name=both, split_axis=0, concat_axis=0, tiled=True
    )
    total_rows = float(weight.shape[0] * 16)
    weight_rows = weight.reshape(-1, LANES)
    starts = (0, 16, 8, 24)
    places = [8 * starts.index(i // 8 * 8) + i % 8 for i in range(NF // 2)]
    parts, high, low = gram_parts(snapshots, weight_rows, total_rows, places)

    group = lax.axis_index("freq")
    place = lax.axis_index("pts")
    first = (group * 16 + lax.rem(place, 2) * 8 + lax.div(place, 2)) * 2
    start_pair = lax.dynamic_slice_in_dim(start_vec, first, 2, 0)
    start_pair = jnp.transpose(start_pair, (1, 2, 0))[:, :, :, None]
    start_pair = jnp.broadcast_to(start_pair, (2, NB, 2, NB)).reshape(2, NB, 2 * NB)
    start_pair = jnp.concatenate([start_pair, start_pair], axis=2)

    parts = exchange(parts, axis_index_groups=near).reshape(4, 8, NB // 2, LANES)
    parts = small_call(near_sum_kernel, "near_sum", floats(8, NB // 2, LANES))(parts)
    parts = exchange(parts, axis_index_groups=far)
    own = small_call(far_sum_kernel, "far_sum", floats(8, NB // 2 + 8, LANES))(parts, start_pair)
    own = exchange(own, axis_index_groups=far)
    response, packed = small_call(
        far_join_kernel, "far_join", (floats(4, 8, LANES), floats(8, NB // 2, LANES))
    )(own)
    response = exchange(response, axis_index_groups=near)
    other = lax.ppermute(packed, both, [(i, i ^ 2) for i in range(n_devices)])
    gram_mine = unpack_gram(packed, other)
    modes = local_modes(high, low, weight_rows, response, starts, total_rows, 2)
    got = lax.ppermute(modes[1], "freq", [(0, 1), (1, 0)])
    return gram_mine, join_modes(modes, got)


def shards(n_pts, n_freq, snapshots, weight, start_vec):
    cols = snapshots.shape[1]
    total_rows = float(weight.shape[0] * n_pts)
    n_devices = n_pts * n_freq
    mine_count = NF // n_freq
    group = lax.axis_index("freq")
    weight_rows = weight.reshape(-1, LANES)
    parts, high, low = gram_parts(snapshots, weight_rows, total_rows, list(range(NF // 2)))
    share = parts.reshape(n_devices, -1)
    share = jnp.sum(lax.all_to_all(share, ("freq", "pts"), 0, 0, tiled=True), axis=0)
    packed = lax.all_gather(share, "pts", axis=0, tiled=True)
    gram_mine = unpack_gram(packed.reshape(mine_count // 2, NB // 2, LANES))
    start_mine = lax.dynamic_slice_in_dim(start_vec, group * mine_count, mine_count, 0)
    response = lax.all_gather(response_of(gram_mine, start_mine), "freq", axis=0, tiled=True)
    response = jnp.transpose(response.reshape(NF // 2, 2, 2, NB), (0, 2, 1, 3))
    response = response.reshape(1, NF // 2, LANES)
    modes = local_modes(high, low, weight_rows, response, (0,), total_rows, n_freq)
    modes = lax.all_to_all(modes, "freq", 0, 0, tiled=True)
    modes = modes.reshape(n_freq, cols // LANES, 2, mine_count, LANES)
    modes = jnp.transpose(modes, (3, 2, 0, 1, 4)).reshape(mine_count, 2, n_freq * cols)
    return gram_mine, modes


def solution(mesh):
    n_pts, n_freq = mesh.shape["pts"], mesh.shape["freq"]
    if (n_pts, n_freq) == (16, 2):
        body = functools.partial(two_level_shards, n_pts * n_freq)
    else:
        body = functools.partial(shards, n_pts, n_freq)
    placed = (P(None, ("pts", "freq")), P("pts"), P())
    return jax.shard_map(
        body,
        mesh=mesh,
        in_specs=placed,
        out_specs=(P("freq", None, None, None), P("freq", None, "pts")),
        check_vma=False,
    )
```

time: 67.8 us -> 64.2 us (0.947)
  starting transfers between devices: 28.8 us -> 10.7 us
  blocking collectives: 0 us -> 16.4 us
  local copies, waits for them, and re-layouts: 4.01 us -> 2.15 us
    ppermute x22 -> x2, starting transfers between devices: 28.8 us -> 0.07 us  [the longest x1 0.07 us: two_level_shards(): other = lax.ppermute(packed, both, [(i, i ^ 2) for i in range(n_devices)])]
    all_to_all x0 -> x2, blocking collectives: none -> 16.4 us  [the longest x1 9.52 us: two_level_shards(): own = exchange(own, axis_index_groups=far)]
    ppermute x22 -> x2, waiting for transfers between devices: 15.6 us -> 2.83 us  [the longest x1 1.59 us: two_level_shards(): got = lax.ppermute(modes[1], 'freq', [(0, 1), (1, 0)])]
    all_to_all x0 -> x2, waiting for transfers between devices: none -> 12.5 us  [the longest x1 6.5 us: two_level_shards(): parts = exchange(parts, axis_index_groups=far)]
    all_to_all x0 -> x2, starting transfers between devices: none -> 10.6 us  [the longest x1 6.39 us: two_level_shards(): parts = exchange(parts, axis_index_groups=far)]
    unnamed x12 -> x4, local copies, waits for them, and re-layouts: 3.7 us -> 0.94 us
    squeeze x1, local copies, waits for them, and re-layouts: 0.01 us -> 0.9 us  [two_level_shards(): got = lax.ppermute(modes[1], 'freq', [(0, 1), (1, 0)])]
    pallas_call x2, Pallas kernels: 14.3 us -> 15 us  [the longest x1 11.1 us: gram_parts(): pl.pallas_call(functools.partial(gram_kernel, total_rows, places), out_sh...]
  transfers between devices with their start and end apart: 22 -> 4, of which waited for: 10 -> 4; matrix products, arithmetic and copies ran while one was open for 1% -> 1% of each run, Pallas kernels for 4% -> 3%
where the time goes in v1:
time: 64.2 us; the launch traced here: 63.8 us
  Pallas kernels  18.4 us (29%)
  blocking collectives  16.4 us (26%)
  waiting for transfers between devices  15.4 us (24%)
  starting transfers between devices  10.7 us (17%)
  local copies, waits for them, and re-layouts  2.15 us (3%)
  between operations  0.69 us (1%)
    pallas_call x1, Pallas kernels, gram_parts(): pl.pallas_call(functools.partial(gram_kernel, total_rows, places), out_sh...  11.1 us
    all_to_all x1, blocking collectives, two_level_shards(): own = exchange(own, axis_index_groups=far)  9.52 us
    all_to_all x1, blocking collectives, two_level_shards(): response = exchange(response, axis_index_groups=near)  6.88 us
    all_to_all x1, waiting for transfers between devices, two_level_shards(): parts = exchange(parts, axis_index_groups=far)  6.5 us
    all_to_all x1, starting transfers between devices, two_level_shards(): parts = exchange(parts, axis_index_groups=far)  6.39 us
    all_to_all x1, waiting for transfers between devices, two_level_shards(): exchange(parts, axis_index_groups=near).reshape(4, 8, NB // 2, LANES)  6.04 us
    all_to_all x1, starting transfers between devices, two_level_shards(): exchange(parts, axis_index_groups=near).reshape(4, 8, NB // 2, LANES)  4.21 us
    pallas_call x1, Pallas kernels, local_modes(): pl.pallas_call(functools.partial(modes_kernel, total_rows, starts), out_s...  3.91 us
  transfers between devices with their start and end apart: 4, of which 4 were waited for; matrix products, arithmetic and copies ran while one was open for 1% of the time, Pallas kernels for 3%

profile of v1, /device:TPU:0, one launch (start us, length us, event | category | flops | bytes accessed | tf_op | source)
XLA Modules:
  0.0 63.8 jit_solution(5521210665133119814)
XLA Ops:
  0.6 0.0 copy-start
  0.6 11.1 %gram_parts.1 = (f32[32,16,128]{2,1,0:T(8,128)}, bf16[2112,384]{1,0:T(8,128)(2,1)}, bf16[2112,384]{1,0:T(8,128)(2,1)}) custom-call(f32[2112,384]{1,0:T(8,128)} %x_hbm.1, f32[6,128]{1,0:T(8,128)} %bitcast.7, bf16[256,256]{1,0:T(8,128)(2,1)} %constant.27.clone.dft_hbm), custom_call_target="tpu_custom_call" | custom-call | flops 5000000000 | bytes 8000000 | tf_op jit(solution)/shard_map/gram_parts/pallas_call | solution.py:231
  11.7 4.2 %all-to-all-start = ((f32[32,16,128]{2,1,0:T(8,128)}), f32[32,16,128]{2,1,0:T(8,128)S(1)}, u32[]{:S(2)}, u32[]{:S(2)}) async-start(f32[32,16,128]{2,1,0:T(8,128)} %get-tuple-element.7), calls=%async_computation | async-start | bytes 524288 | tf_op jit(solution)/shard_map/all_to_all | solution.py:497
  15.9 6.0 %all-to-all-done = f32[32,16,128]{2,1,0:T(8,128)S(1)} async-done(((f32[32,16,128]{2,1,0:T(8,128)}), f32[32,16,128]{2,1,0:T(8,128)S(1)}, u32[]{:S(2)}, u32[]{:S(2)}) %all-to-all-start) | async-done | bytes 262176 | tf_op jit(solution)/shard_map/all_to_all | solution.py:497
  22.0 0.6 %near_sum.1 = f32[8,16,128]{2,1,0:T(8,128)} custom-call(f32[4,8,16,128]{3,2,1,0:T(8,128)S(1)} %bitcast.6), custom_call_target="tpu_custom_call" | custom-call | tf_op jit(solution)/shard_map/near_sum/pallas_call | solution.py:272
  22.6 6.4 %all-to-all-start.1 = ((f32[8,16,128]{2,1,0:T(8,128)}), f32[8,16,128]{2,1,0:T(8,128)S(1)}, u32[]{:S(2)}, u32[]{:S(2)}) async-start(f32[8,16,128]{2,1,0:T(8,128)} %near_sum.1), calls=%async_computation.1 | async-start | bytes 131072 | tf_op jit(solution)/shard_map/all_to_all | solution.py:499
  29.0 0.0 copy-done
  29.0 0.1 dynamic-slice_bitcast_fusion
  29.1 0.1 broadcast_in_dim.2
  29.2 0.1 reshape.16
  29.3 0.1 pad_maximum_fusion.start_ref
  29.4 6.5 %all-to-all-done.1.parts_ref = f32[8,16,128]{2,1,0:T(8,128)S(1)} async-done(((f32[8,16,128]{2,1,0:T(8,128)}), f32[8,16,128]{2,1,0:T(8,128)S(1)}, u32[]{:S(2)}, u32[]{:S(2)}) %all-to-all-start.1) | async-done | bytes 65568 | tf_op jit(solution)/shard_map/all_to_all | solution.py:499
  35.9 0.3 far_sum.1
  36.2 9.5 %all_to_all.20.parts_ref = f32[8,24,128]{2,1,0:T(8,128)S(1)} all-to-all(f32[8,24,128]{2,1,0:T(8,128)S(1)} %far_sum.1), channel_id=1, replica_groups={{0,4,8,12,16,20,24,28},{1,5,9,13,17,21,25,29},{2,6,10,14,18,22,26,30},{..., dimensions={0} | all-to-all | bytes 196608 | tf_op jit(solution)/shard_map/all_to_all | solution.py:501
  45.7 6.9 %all_to_all.21.resp_hbm = f32[4,8,128]{2,1,0:T(8,128)} all-to-all(f32[4,8,128]{2,1,0:T(8,128)S(1)} %get-tuple-element.11), channel_id=1, replica_groups={{0,1,2,3},{4,5,6,7},{8,9,10,11},{12,13,14,15},{16,17,18,19},{20,21,22,2..., dimensions={0} | all-to-all | bytes 32768 | tf_op jit(solution)/shard_map/all_to_all | solution.py:505
  52.6 3.9 %local_modes.1.kept_ref = f32[2,6,32,128]{3,2,1,0:T(8,128)} custom-call(bf16[2112,384]{1,0:T(8,128)(2,1)} %get-tuple-element.9.high_hbm, bf16[2112,384]{1,0:T(8,128)(2,1)} %get-tuple-element.10.low_hbm, f32[6,128]{1,0:T(8,128)} %bitcast.8, f32[2,128,128]{2,1,0:T(8,128)} %constant.28.clone.table_hbm, f32[4,8,128]{2,1,0:T(8,128)} %all_to_all.21.resp_hbm), custom_call_target="tpu_custom_call" | custom-call | tf_op jit(solution)/shard_map/local_modes/pallas_call | solution.py:432
  56.5 0.9 %slice_bitcast_fusion = f32[6,32,128]{2,1,0:T(8,128)S(1)} fusion(f32[2,6,32,128]{3,2,1,0:T(8,128)} %local_modes.1.kept_ref), kind=kLoop, calls=%fused_computation | loop fusion | bytes 196608 | tf_op jit(solution)/shard_map/squeeze | solution.py:509
  57.4 0.0 collective-permute-start.1
  57.5 0.1 collective-permute-start
  57.5 1.2 %collective-permute-done.refs_1_ = f32[8,16,128]{2,1,0:T(8,128)S(1)} collective-permute-done((f32[8,16,128]{2,1,0:T(8,128)S(1)}, f32[8,16,128]{2,1,0:T(8,128)S(1)}, u32[]{:S(2)}, u32[]{:S(2)}) %collective-permute-start) | collective-permute-done | bytes 65568 | tf_op jit(solution)/shard_map/ppermute | solution.py:506
  58.8 1.7 %unpack_gram.1 = f32[32,2,32,32]{3,2,1,0:T(8,128)} custom-call(f32[8,16,128]{2,1,0:T(8,128)S(1)} %get-tuple-element.8.refs_0_, f32[8,16,128]{2,1,0:T(8,128)S(1)} %collective-permute-done.refs_1_), custom_call_target="tpu_custom_call" | custom-call | tf_op jit(solution)/shard_map/unpack_gram/pallas_call | solution.py:272
  60.5 1.6 %collective-permute-done.1.got_ref = f32[6,32,128]{2,1,0:T(8,128)S(1)} collective-permute-done((f32[6,32,128]{2,1,0:T(8,128)S(1)}, f32[6,32,128]{2,1,0:T(8,128)S(1)}, u32[]{:S(2)}, u32[]{:S(2)}) %collective-permute-start.1) | collective-permute-done | bytes 98336 | tf_op jit(solution)/shard_map/ppermute | solution.py:509
  62.1 0.0 copy-start.1
  62.1 0.9 %copy-done.1 = f32[2,6,32,128]{3,2,1,0:T(8,128)S(1)} copy-done((f32[2,6,32,128]{3,2,1,0:T(8,128)S(1)}, f32[2,6,32,128]{3,2,1,0:T(8,128)}, u32[]{:S(2)}) %copy-start.1) | copy-done | bytes 196632
  63.0 0.8 %join_modes.1 = f32[32,2,768]{2,1,0:T(2,128)} custom-call(f32[2,6,32,128]{3,2,1,0:T(8,128)S(1)} %copy-done.1, f32[6,32,128]{2,1,0:T(8,128)S(1)} %collective-permute-done.1.got_ref), custom_call_target="tpu_custom_call" | custom-call | tf_op jit(solution)/shard_map/join_modes/pallas_call | solution.py:272
  (1 shorter events, 0.0 us)
Async XLA Ops:
  0.6 28.4 %copy-start = (f32[64,2,32]{0,2,1:T(8,128)S(1)}, f32[64,2,32]{0,2,1:T(8,128)}, u32[]{:S(2)}) copy-start(f32[64,2,32]{0,2,1:T(8,128)} %param.7) | copy-start | bytes 49156
  11.7 10.2 %all-to-all-start = ((f32[32,16,128]{2,1,0:T(8,128)}), f32[32,16,128]{2,1,0:T(8,128)S(1)}, u32[]{:S(2)}, u32[]{:S(2)}) async-start(f32[32,16,128]{2,1,0:T(8,128)} %get-tuple-element.7), calls=%async_computation | async-start | bytes 524288 | tf_op jit(solution)/shard_map/all_to_all | solution.py:497
  22.6 13.3 %all-to-all-start.1 = ((f32[8,16,128]{2,1,0:T(8,128)}), f32[8,16,128]{2,1,0:T(8,128)S(1)}, u32[]{:S(2)}, u32[]{:S(2)}) async-start(f32[8,16,128]{2,1,0:T(8,128)} %near_sum.1), calls=%async_computation.1 | async-start | bytes 131072 | tf_op jit(solution)/shard_map/all_to_all | solution.py:499
  57.4 4.6 %collective-permute-start.1 = (f32[6,32,128]{2,1,0:T(8,128)S(1)}, f32[6,32,128]{2,1,0:T(8,128)S(1)}, u32[]{:S(2)}, u32[]{:S(2)}) collective-permute-start(f32[6,32,128]{2,1,0:T(8,128)S(1)} %slice_bitcast_fusion), channel_id=1, source_target_pairs={{0,1},{1,0},{2,3},{3,2},{4,5},{5,4},{6,7},{7,6},{8,9},{9,8},{10,11... | collective-permute-start | bytes 294920 | tf_op jit(solution)/shard_map/ppermute | solution.py:509
  57.5 1.3 %collective-permute-start = (f32[8,16,128]{2,1,0:T(8,128)S(1)}, f32[8,16,128]{2,1,0:T(8,128)S(1)}, u32[]{:S(2)}, u32[]{:S(2)}) collective-permute-start(f32[8,16,128]{2,1,0:T(8,128)S(1)} %get-tuple-element.8.refs_0_), channel_id=1, source_target_pairs={{0,2},{1,3},{2,0},{3,1},{4,6},{5,7},{6,4},{7,5},{8,10},{9,11},{10,... | collective-permute-start | bytes 196616 | tf_op jit(solution)/shard_map/ppermute | solution.py:506
  62.1 0.9 %copy-start.1 = (f32[2,6,32,128]{3,2,1,0:T(8,128)S(1)}, f32[2,6,32,128]{3,2,1,0:T(8,128)}, u32[]{:S(2)}) copy-start(f32[2,6,32,128]{3,2,1,0:T(8,128)} %local_modes.1.kept_ref) | copy-start | bytes 589828
